TPU v7x, 256 devices: a whole 4x4x8 slice. The times are simulated.
256 devices in a mesh: leaf: 32 (over z, x), panel: 8 (over y, core).
Axes of the slice: x: 4, y: 4, z: 8, core: 2. Of those that a mesh axis runs over, the one named last changes fastest.
Arguments:
- leaf_sides: bfloat16 [65536, 128], P(('leaf', 'panel')), may hold values from -6 to 6
- leaf_inverse: bfloat16 [65536, 2048], P(('leaf', 'panel')), may hold values from -0.1875 to 0.1875
- leaf_panels: bfloat16 [3, 4096, 65536], P(None, 'panel', 'leaf'), may hold values from -0.125 to 0.125
- parent_map: int32 [32], P('leaf'), may hold values from 0 to 3, as said below
- tile_mask: int32 [32, 3, 32], P('leaf'), may hold values 0 or 1
- top_sides: bfloat16 [7, 4096, 128], P(None, ('panel', 'leaf')), may hold values from -6 to 6
- grand_inverse: bfloat16 [16384, 4096], P('leaf', 'panel'), may hold values from -0.125 to 0.125
- child_inverse: bfloat16 [8192, 4096], P('leaf', 'panel'), may hold values from -0.125 to 0.125
- root_inverse: bfloat16 [4096, 4096], P('leaf', 'panel'), may hold values from -0.125 to 0.125
- child_panels: bfloat16 [4096, 16384], P('panel', 'leaf'), may hold values from -0.09375 to 0.09375
- root_grand: bfloat16 [4096, 16384], P('panel', 'leaf'), may hold values from -0.09375 to 0.09375
- root_child: bfloat16 [4096, 8192], P('panel', 'leaf'), may hold values from -0.09375 to 0.09375
Outputs:
- leaf_solution: bfloat16 [65536, 128], P(('leaf', 'panel'))
- top_solution: bfloat16 [7, 4096, 128], P(None, ('panel', 'leaf'))
Inputs may be any that keep to these rules, and one draw needn't show every extreme that they name: `parent_map`: each of the 4 grandchild separators is the parent of at least one subtree.
All inputs are finite; a program needn't handle non-finite values. No bound on the sum of `tile_mask` on one device may be relied on, other than what follows from the above.
Results may differ from a plain program's by a relative error of at most 0.017.
Values may be sent and summed in bfloat16 or wider, within the bound.
A program may use at most 64 MiB of HBM per device.

v0:
```python
import jax
import jax.numpy as jnp
from jax import lax
from jax.sharding import PartitionSpec as P

TILE_ROWS = 128


def lower_part(matrix, row_offset, col_offset):
    row_index = row_offset + lax.broadcasted_iota(jnp.int32, matrix.shape, 0)
    col_index = col_offset + lax.broadcasted_iota(jnp.int32, matrix.shape, 1)
    return jnp.where(row_index >= col_index, matrix, jnp.zeros_like(matrix))


def fold_rows(portions, step_rule, initial):
    return step_rule(initial, lax.all_gather(portions, "panel", axis=0, tiled=True), jnp.int32(0))


def reduce_rows(partial_value):
    return lax.psum_scatter(partial_value, "panel", scatter_dimension=0, tiled=True)


def level_total(partial_value):
    return lax.psum(partial_value, "leaf").astype(jnp.bfloat16)


def forward_rule(matrix):

    def forward_apply_rule(running, portion, offset):
        return jnp.dot(matrix, portion, preferred_element_type=jnp.float32)

    return forward_apply_rule


def transpose_product(matrix, vectors):
    return lax.dot_general(
        matrix, vectors, (((0,), (0,)), ((), ())), preferred_element_type=jnp.float32
    )


def backward_rule(matrix):

    def backward_apply_rule(running, portion, offset):
        return transpose_product(matrix, portion)

    return backward_apply_rule


def per_device(
    leaf_sides,
    leaf_inverse,
    leaf_panels,
    parent_map,
    tile_mask,
    top_sides,
    grand_inverse,
    child_inverse,
    root_inverse,
    child_panels,
    root_grand,
    root_child,
):
    leaf_index = lax.axis_index("leaf")
    panel_index = lax.axis_index("panel")
    part_rows = leaf_sides.shape[0]
    side_count = leaf_sides.shape[1]
    slice_rows = leaf_panels.shape[1]
    separator = slice_rows * lax.axis_size("panel")
    share_rows = top_sides.shape[1]
    leaf_lower = lower_part(leaf_inverse, panel_index * part_rows, 0)
    solved_leaf = fold_rows(
        leaf_sides, forward_rule(leaf_lower), jnp.zeros((part_rows, side_count), jnp.float32)
    ).astype(jnp.bfloat16)

    def leaf_update(running, portion, offset):
        return jnp.einsum("kin,nr->kir", leaf_panels, portion, preferred_element_type=jnp.float32)

    updates = fold_rows(
        solved_leaf, leaf_update, jnp.zeros((3, slice_rows, side_count), jnp.float32)
    )
    tile_count = slice_rows // TILE_ROWS
    tile_rows = lax.dynamic_slice_in_dim(tile_mask[0], panel_index * tile_count, tile_count, 1)
    row_mask = jnp.repeat(tile_rows.astype(jnp.float32), TILE_ROWS, axis=1)
    updates = updates * row_mask[:, :, None]
    parent = parent_map[0]
    grand_slots = (jnp.arange(4, dtype=jnp.int32) == parent).astype(jnp.float32)
    child_slots = (jnp.arange(2, dtype=jnp.int32) == parent // 2).astype(jnp.float32)

    def placed(side_rows):
        empty_rows = jnp.zeros((side_rows.shape[0], slice_rows, side_count), jnp.float32)
        return lax.dynamic_update_slice_in_dim(
            empty_rows, side_rows.astype(jnp.float32), leaf_index * share_rows, 1
        )

    grand_owners = separator // grand_inverse.shape[0]
    grand_node = leaf_index // grand_owners
    own_grand = (jnp.arange(4, dtype=jnp.int32) == grand_node).astype(jnp.float32)
    grand_lower = lower_part(
        grand_inverse, leaf_index % grand_owners * grand_inverse.shape[0], panel_index * slice_rows
    )
    grand_sums = level_total(placed(top_sides[0:4]) - grand_slots[:, None, None] * updates[0][None])
    grand_right = lax.dynamic_index_in_dim(grand_sums, grand_node, 0, keepdims=False)
    grand_solved = reduce_rows(
        jnp.dot(grand_lower, grand_right, preferred_element_type=jnp.float32)
    ).astype(jnp.bfloat16)

    def grand_update(running, portion, offset):
        return jnp.stack(
            [
                jnp.dot(child_panels, portion, preferred_element_type=jnp.float32),
                jnp.dot(root_grand, portion, preferred_element_type=jnp.float32),
            ]
        )

    from_grand = fold_rows(
        grand_solved, grand_update, jnp.zeros((2, slice_rows, side_count), jnp.float32)
    )
    child_owners = separator // child_inverse.shape[0]
    child_node = leaf_index // child_owners
    own_child = (jnp.arange(2, dtype=jnp.int32) == child_node).astype(jnp.float32)
    child_lower = lower_part(
        child_inverse, leaf_index % child_owners * child_inverse.shape[0], panel_index * slice_rows
    )
    child_terms = (
        placed(top_sides[4:6])
        - child_slots[:, None, None] * updates[1][None]
        - own_child[:, None, None] * from_grand[0][None]
    )
    child_sums = level_total(child_terms)
    child_right = lax.dynamic_index_in_dim(child_sums, child_node, 0, keepdims=False)
    child_solved = reduce_rows(
        jnp.dot(child_lower, child_right, preferred_element_type=jnp.float32)
    ).astype(jnp.bfloat16)
    from_child = fold_rows(
        child_solved, forward_rule(root_child), jnp.zeros((slice_rows, side_count), jnp.float32)
    )
    root_terms = placed(top_sides[6:7]) - (updates[2] + from_grand[1] + from_child)[None]
    root_right = level_total(root_terms)[0]
    root_lower = lower_part(
        root_inverse, leaf_index * root_inverse.shape[0], panel_index * slice_rows
    )
    root_solved = reduce_rows(
        jnp.dot(root_lower, root_right, preferred_element_type=jnp.float32)
    ).astype(jnp.bfloat16)
    blank_slice = jnp.zeros((slice_rows, side_count), jnp.float32)
    root_result = level_total(fold_rows(root_solved, backward_rule(root_lower), blank_slice)[None])[
        0
    ]
    child_residual = (
        child_solved.astype(jnp.float32) - reduce_rows(transpose_product(root_child, root_result))
    ).astype(jnp.bfloat16)
    child_part = fold_rows(child_residual, backward_rule(child_lower), blank_slice)
    child_result = level_total(own_child[:, None, None] * child_part[None])
    child_mine = lax.dynamic_index_in_dim(child_result, child_node, 0, keepdims=False)
    grand_back = transpose_product(child_panels, child_mine) + transpose_product(
        root_grand, root_result
    )
    grand_residual = (grand_solved.astype(jnp.float32) - reduce_rows(grand_back)).astype(
        jnp.bfloat16
    )
    grand_part = fold_rows(grand_residual, backward_rule(grand_lower), blank_slice)
    grand_result = level_total(own_grand[:, None, None] * grand_part[None])
    ancestors = jnp.stack(
        [
            lax.dynamic_index_in_dim(grand_result, parent, 0, keepdims=False),
            lax.dynamic_index_in_dim(child_result, parent // 2, 0, keepdims=False),
            root_result,
        ]
    )
    ancestors = ancestors * row_mask[:, :, None].astype(jnp.bfloat16)
    pulled = jnp.einsum("kin,kir->nr", leaf_panels, ancestors, preferred_element_type=jnp.float32)
    leaf_residual = (solved_leaf.astype(jnp.float32) - reduce_rows(pulled)).astype(jnp.bfloat16)
    leaf_result = reduce_rows(transpose_product(leaf_lower, leaf_residual))
    leaf_solution = leaf_result.astype(jnp.bfloat16)
    top_all = jnp.concatenate([grand_result, child_result, root_result[None]], axis=0)
    top_solution = lax.dynamic_slice_in_dim(top_all, leaf_index * share_rows, share_rows, 1)
    return (leaf_solution, top_solution)


def solution(mesh):
    placed = (
        P(("leaf", "panel"), None),
        P(("leaf", "panel"), None),
        P(None, "panel", "leaf"),
        P("leaf"),
        P("leaf", None, None),
        P(None, ("panel", "leaf"), None),
        P("leaf", "panel"),
        P("leaf", "panel"),
        P("leaf", "panel"),
        P("panel", "leaf"),
        P("panel", "leaf"),
        P("panel", "leaf"),
    )
    return jax.shard_map(
        per_device,
        mesh=mesh,
        in_specs=placed,
        out_specs=(P(("leaf", "panel"), None), P(None, ("panel", "leaf"), None)),
        check_vma=False,
    )
```

profile of v0, /device:TPU:1, one launch (start us, length us, event | category | flops | bytes accessed | tf_op | source)
XLA Modules:
  0.0 1237.5 jit_solution(8591428646694366444)
XLA Ops:
  7.3 0.8 fusion.37
  8.2 16.4 %all_gather.21 = bf16[2048,128]{1,0:T(8,128)(2,1)S(1)} all-gather(bf16[256,128]{1,0:T(8,128)(2,1)} %param.12), channel_id=1, replica_groups=mesh['leaf'=32,'panel'=8] {'panel'}, dimensions={0}, use_global_device_ids=true | all-gather | bytes 589824 | tf_op jit(solution)/shard_map/all_gather | solution.py:16
  24.6 1.7 convolution_convert_fusion
  26.3 13.1 %all_gather.22 = bf16[2048,128]{1,0:T(8,128)(2,1)S(1)} all-gather(bf16[256,128]{1,0:T(8,128)(2,1)S(1)} %convolution_convert_fusion), channel_id=1, replica_groups=mesh['leaf'=32,'panel'=8] {'panel'}, dimensions={0}, use_global_device_ids=true | all-gather | bytes 589824 | tf_op jit(solution)/shard_map/all_gather | solution.py:16
  39.4 5.0 fusion.1
  44.5 0.7 slice_bitcast_fusion.1
  46.3 129.3 %all-reduce.6 = bf16[4,512,128]{2,1,0:T(8,128)(2,1)} all-reduce(f32[4,512,128]{2,1,0:T(8,128)S(1)} %multiply_subtract_fusion), channel_id=1, replica_groups=mesh['leaf'=32,'panel'=8] {'leaf'}, use_global_device_ids=true, to_apply=%region_0.1 | all-reduce | flops 262144 | bytes 1572864 | tf_op jit(solution)/shard_map/psum | solution.py:24
  175.6 2.1 fusion.17
  177.8 1.1 copy.16
  178.9 0.5 compare_convert_fusion
  179.5 0.6 iota_add_fusion.2
  180.1 49.0 %reduce-scatter.8.cloned.1.call-done = f32[64,128]{1,0:T(8,128)} async-done(((f32[512,128]{1,0:T(8,128)}), f32[64,128]{1,0:T(8,128)}) %reduce-scatter.8.cloned.1.call-update) | async-done | bytes 32784 | tf_op jit(solution)/shard_map/reduce_scatter | solution.py:20
  229.1 0.8 convert_element_type.110
  229.8 15.6 %all_gather.23 = bf16[512,128]{1,0:T(8,128)(2,1)S(1)} all-gather(bf16[64,128]{1,0:T(8,128)(2,1)S(1)} %convert_element_type.110), channel_id=1, replica_groups=mesh['leaf'=32,'panel'=8] {'panel'}, dimensions={0}, use_global_device_ids=true | all-gather | bytes 147456 | tf_op jit(solution)/shard_map/all_gather | solution.py:16
  245.7 0.8 copy.17
  246.6 1.1 multiply_subtract_fusion.1
  247.7 120.2 %all-reduce.7 = bf16[2,512,128]{2,1,0:T(8,128)(2,1)S(1)} all-reduce(f32[2,512,128]{2,1,0:T(8,128)S(1)} %multiply_subtract_fusion.1), channel_id=1, replica_groups=mesh['leaf'=32,'panel'=8] {'leaf'}, use_global_device_ids=true, to_apply=%region_2.3 | all-reduce | flops 131072 | bytes 786432 | tf_op jit(solution)/shard_map/psum | solution.py:24
  367.9 1.9 fusion.21
  369.9 0.7 slice_convert_fusion
  370.7 0.7 dynamic_update_slice.11
  371.4 50.6 %reduce-scatter.10.cloned.1.call-done = f32[32,128]{1,0:T(8,128)} async-done(((f32[256,128]{1,0:T(8,128)}), f32[32,128]{1,0:T(8,128)}) %reduce-scatter.10.cloned.1.call-update) | async-done | bytes 16400 | tf_op jit(solution)/shard_map/reduce_scatter | solution.py:20
  422.1 0.7 convert_element_type.116
  422.8 15.5 %all_gather.24 = bf16[256,128]{1,0:T(8,128)(2,1)S(1)} all-gather(bf16[32,128]{1,0:T(8,128)(2,1)S(1)} %convert_element_type.116), channel_id=1, replica_groups=mesh['leaf'=32,'panel'=8] {'panel'}, dimensions={0}, use_global_device_ids=true | all-gather | bytes 73728 | tf_op jit(solution)/shard_map/all_gather | solution.py:16
  438.9 116.7 %all-reduce.8 = bf16[1,512,128]{1,2,0:T(8,128)(2,1)S(1)} all-reduce(f32[1,512,128]{1,2,0:T(8,128)S(1)} %fusion.6), channel_id=1, replica_groups=mesh['leaf'=32,'panel'=8] {'leaf'}, use_global_device_ids=true, to_apply=%region_4.5 | all-reduce | flops 65536 | bytes 393216 | tf_op jit(solution)/shard_map/psum | solution.py:24
  555.6 1.8 fusion.27
  557.5 52.3 %reduce-scatter.12.cloned.1.call-done = f32[16,128]{1,0:T(8,128)} async-done(((f32[128,128]{1,0:T(8,128)}), f32[16,128]{1,0:T(8,128)}) %reduce-scatter.12.cloned.1.call-update) | async-done | bytes 8208 | tf_op jit(solution)/shard_map/reduce_scatter | solution.py:20
  609.8 0.7 convert_element_type.120
  610.5 15.6 %all_gather.25 = bf16[128,128]{1,0:T(8,128)(2,1)S(1)} all-gather(bf16[16,128]{1,0:T(8,128)(2,1)S(1)} %convert_element_type.120), channel_id=1, replica_groups=mesh['leaf'=32,'panel'=8] {'panel'}, dimensions={0}, use_global_device_ids=true | all-gather | bytes 36864 | tf_op jit(solution)/shard_map/all_gather | solution.py:16
  626.1 1.2 convolution_bitcast_fusion.3
  627.3 117.0 %all-reduce.9 = bf16[1,512,128]{2,1,0:T(8,128)(2,1)S(1)} all-reduce(f32[1,512,128]{2,1,0:T(8,128)S(1)} %convolution_bitcast_fusion.3), channel_id=1, replica_groups=mesh['leaf'=32,'panel'=8] {'leaf'}, use_global_device_ids=true, to_apply=%region_6.7 | all-reduce | flops 65536 | bytes 393216 | tf_op jit(solution)/shard_map/psum | solution.py:24
  744.3 0.9 convolution_bitcast_fusion.5
  745.3 52.2 %reduce-scatter.14.cloned.1.call-done = f32[32,128]{1,0:T(8,128)} async-done(((f32[256,128]{1,0:T(8,128)}), f32[32,128]{1,0:T(8,128)}) %reduce-scatter.14.cloned.1.call-update) | async-done | bytes 16400 | tf_op jit(solution)/shard_map/reduce_scatter | solution.py:20
  797.5 0.7 subtract_convert_fusion.3
  798.2 15.6 %all_gather.26 = bf16[256,128]{1,0:T(8,128)(2,1)S(1)} all-gather(bf16[32,128]{1,0:T(8,128)(2,1)S(1)} %subtract_convert_fusion.3), channel_id=1, replica_groups=mesh['leaf'=32,'panel'=8] {'panel'}, dimensions={0}, use_global_device_ids=true | all-gather | bytes 73728 | tf_op jit(solution)/shard_map/all_gather | solution.py:16
  813.8 1.3 fusion.31
  815.2 120.1 %all-reduce.10 = bf16[2,512,128]{2,1,0:T(8,128)(2,1)S(1)} all-reduce(f32[2,512,128]{2,1,0:T(8,128)S(1)} %broadcast_multiply_fusion.1), channel_id=1, replica_groups=mesh['leaf'=32,'panel'=8] {'leaf'}, use_global_device_ids=true, to_apply=%region_8.9 | all-reduce | flops 131072 | bytes 786432 | tf_op jit(solution)/shard_map/psum | solution.py:24
  935.7 1.0 fusion.2
  936.9 52.3 %reduce-scatter.16.cloned.1.call-done = f32[64,128]{1,0:T(8,128)} async-done(((f32[512,128]{1,0:T(8,128)}), f32[64,128]{1,0:T(8,128)}) %reduce-scatter.16.cloned.1.call-update) | async-done | bytes 32784 | tf_op jit(solution)/shard_map/reduce_scatter | solution.py:20
  989.2 0.8 subtract_convert_fusion.2
  990.0 15.5 %all_gather.27 = bf16[512,128]{1,0:T(8,128)(2,1)S(1)} all-gather(bf16[64,128]{1,0:T(8,128)(2,1)S(1)} %subtract_convert_fusion.2), channel_id=1, replica_groups=mesh['leaf'=32,'panel'=8] {'panel'}, dimensions={0}, use_global_device_ids=true | all-gather | bytes 147456 | tf_op jit(solution)/shard_map/all_gather | solution.py:16
  1005.5 0.5 fusion.16
  1006.2 127.5 %all-reduce.11 = bf16[4,512,128]{2,1,0:T(8,128)(2,1)S(1)} all-reduce(f32[4,512,128]{2,1,0:T(8,128)S(1)} %broadcast_multiply_fusion), channel_id=1, replica_groups=mesh['leaf'=32,'panel'=8] {'leaf'}, use_global_device_ids=true, to_apply=%region_10.11 | all-reduce | flops 262144 | bytes 1572864 | tf_op jit(solution)/shard_map/psum | solution.py:24
  1133.7 6.6 convolution_bitcast_fusion
  1140.3 52.6 %reduce-scatter.18.cloned.1.call-done = f32[256,128]{1,0:T(8,128)} async-done(((f32[2048,128]{1,0:T(8,128)}), f32[256,128]{1,0:T(8,128)}) %reduce-scatter.18.cloned.1.call-update) | async-done | bytes 131088 | tf_op jit(solution)/shard_map/reduce_scatter | solution.py:20
  1192.9 2.8 fusion.12
  1195.7 0.6 fusion.33
  1196.3 32.8 %reduce-scatter.20.cloned.1.call-done = f32[256,128]{1,0:T(8,128)} async-done(((f32[2048,128]{1,0:T(8,128)}), f32[256,128]{1,0:T(8,128)}) %reduce-scatter.20.cloned.1.call-update) | async-done | bytes 131088 | tf_op jit(solution)/shard_map/reduce_scatter | solution.py:20
  1229.1 1.5 convert_element_type.128
  (64 shorter events, 2.6 us)
Async XLA Ops:
  7.2 238.3 %copy-start = (bf16[512,512]{1,0:T(8,128)(2,1)S(1)}, bf16[512,512]{1,0:T(8,128)(2,1)}, u32[]{:S(2)}) copy-start(bf16[512,512]{1,0:T(8,128)(2,1)} %param.21) | copy-start | bytes 1572868
  7.2 221.9 %reduce-scatter.8.cloned.1.call-start = ((), (), s32[]{:S(2)}) async-start(), calls=%async_computation.7 | async-start | bytes 294912 | tf_op jit(solution)/shard_map/reduce_scatter | solution.py:20
  7.3 168.3 %copy-start.7 = (s32[512]{0:T(512)}, s32[512]{0:T(512)S(1)}, u32[]{:S(2)}) copy-start(s32[512]{0:T(512)S(1)} %iota_add_fusion.1) | copy-start | bytes 6148
  8.2 37.0 %copy-start.10 = (s32[256]{0:T(256)}, s32[256]{0:T(256)S(1)}, u32[]{:S(2)}) copy-start(s32[256]{0:T(256)S(1)} %iota_add_fusion.3) | copy-start | bytes 3076
  24.6 21.5 %copy-start.6 = (bf16[7,16,128]{2,1,0:T(8,128)(2,1)S(1)}, bf16[7,16,128]{2,1,0:T(8,128)(2,1)}, u32[]{:S(2)}) copy-start(bf16[7,16,128]{2,1,0:T(8,128)(2,1)} %param.17) | copy-start | bytes 86020
  26.3 13.1 %copy-start.4 = (bf16[256,128]{1,0:T(8,128)(2,1)}, bf16[256,128]{1,0:T(8,128)(2,1)S(1)}, u32[]{:S(2)}) copy-start(bf16[256,128]{1,0:T(8,128)(2,1)S(1)} %convolution_convert_fusion) | copy-start | bytes 196612
  46.1 392.2 %copy-start.2 = (bf16[512,256]{1,0:T(8,128)(2,1)S(1)}, bf16[512,256]{1,0:T(8,128)(2,1)}, u32[]{:S(2)}) copy-start(bf16[512,256]{1,0:T(8,128)(2,1)} %param.23) | copy-start | bytes 786436
  46.1 392.4 %copy-start.1 = (bf16[512,512]{1,0:T(8,128)(2,1)S(1)}, bf16[512,512]{1,0:T(8,128)(2,1)}, u32[]{:S(2)}) copy-start(bf16[512,512]{1,0:T(8,128)(2,1)} %param.22) | copy-start | bytes 1572868
  177.7 244.3 %reduce-scatter.10.cloned.1.call-start = ((), (), s32[]{:S(2)}) async-start(), calls=%async_computation.8 | async-start | bytes 147456 | tf_op jit(solution)/shard_map/reduce_scatter | solution.py:20
  247.7 741.6 %copy-start.3 = (f32[64,128]{1,0:T(8,128)S(1)}, f32[64,128]{1,0:T(8,128)}, u32[]{:S(2)}) copy-start(f32[64,128]{1,0:T(8,128)} %reduce-scatter.8.cloned.1.call-done) | copy-start | bytes 98308
  247.7 757.9 %copy-start.8 = (s32[512]{0:T(512)S(1)}, s32[512]{0:T(512)}, u32[]{:S(2)}) copy-start(s32[512]{0:T(512)} %copy-done.7) | copy-start | bytes 6148
  367.9 637.6 %copy-start.9 = (bf16[512,512]{1,0:T(8,128)(2,1)S(1)}, bf16[512,512]{1,0:T(8,128)(2,1)}, u32[]{:S(2)}) copy-start(bf16[512,512]{1,0:T(8,128)(2,1)} %param.18) | copy-start | bytes 1572868
  369.9 239.9 %reduce-scatter.12.cloned.1.call-start = ((), (), s32[]{:S(2)}) async-start(), calls=%async_computation.9 | async-start | bytes 73728 | tf_op jit(solution)/shard_map/reduce_scatter | solution.py:20
  557.4 240.1 %reduce-scatter.14.cloned.1.call-start = ((), (), s32[]{:S(2)}) async-start(), calls=%async_computation.10 | async-start | bytes 147456 | tf_op jit(solution)/shard_map/reduce_scatter | solution.py:20
  745.2 244.0 %reduce-scatter.16.cloned.1.call-start = ((), (), s32[]{:S(2)}) async-start(), calls=%async_computation.11 | async-start | bytes 294912 | tf_op jit(solution)/shard_map/reduce_scatter | solution.py:20
  936.8 256.1 %reduce-scatter.18.cloned.1.call-start = ((), (), s32[]{:S(2)}) async-start(), calls=%async_computation.12 | async-start | bytes 1179648 | tf_op jit(solution)/shard_map/reduce_scatter | solution.py:20
  1006.1 186.7 %copy-start.5 = (bf16[256,128]{1,0:T(8,128)(2,1)S(1)}, bf16[256,128]{1,0:T(8,128)(2,1)}, u32[]{:S(2)}) copy-start(bf16[256,128]{1,0:T(8,128)(2,1)} %copy-done.4) | copy-start | bytes 196612
  1006.2 186.7 %copy-start.11 = (s32[256]{0:T(256)S(1)}, s32[256]{0:T(256)}, u32[]{:S(2)}) copy-start(s32[256]{0:T(256)} %copy-done.10) | copy-start | bytes 3076
  1140.3 88.9 %reduce-scatter.20.cloned.1.call-start = ((), (), s32[]{:S(2)}) async-start(), calls=%async_computation.13 | async-start | bytes 1179648 | tf_op jit(solution)/shard_map/reduce_scatter | solution.py:20
Sparse Core Ops, SparseCore 0:
  177.9 51.1 reduce-scatter.7
  370.0 52.0 reduce-scatter.9
  557.5 52.2 reduce-scatter.11
  745.4 52.0 reduce-scatter.13
  936.9 52.2 reduce-scatter.15
  1140.4 52.4 reduce-scatter.17
  1195.8 33.2 reduce-scatter.19
where the time goes:
time: 1240 us
  blocking collectives  838 us (68%)
  waiting for transfers between devices  342 us (28%)
  matrix products  28.1 us (2%)
  between operations  15.2 us (1%)
    psum x6, blocking collectives, level_total(): return lax.psum(partial_value, 'leaf').astype(jnp.bfloat16)  731 us
    reduce_scatter x7, waiting for transfers between devices, reduce_rows(): lax.psum_scatter(partial_value, 'panel', scatter_dimension=0, tiled=True)  342 us
    all_gather x7, blocking collectives, fold_rows(): lax.all_gather(portions, 'panel', axis=0, tiled=True)  107 us
  transfers between devices with their start and end apart: 7, of which 7 were waited for; matrix products, arithmetic and copies ran while one was open for 0% of the time, Pallas kernels for 0%

commit v1 on v0

v1 whole, which is shorter than its diff:
```python
import functools

import jax
import jax.numpy as jnp
from jax import lax
from jax.experimental import pallas as pl
from jax.experimental.pallas import tpu as pltpu
from jax.sharding import PartitionSpec as P

MESH = pl.DeviceIdType.MESH
F32 = jnp.float32
BF16 = jnp.bfloat16
LEAF = 32
PANEL = 8

(X_SIDES, X_WEIGHT, X_SOLVED, X_U0, X_U12, X_GRIGHT, X_GRED, X_GSOL, X_CTOP, X_CRED, X_CRIGHT, X_CRED2, X_CSOL,
 X_RRED, X_RRIGHT, X_RRED2, X_RSOL, X_RBACK, X_RRES, X_CBACK, X_CRESID, X_CBACK2, X_CRES, X_CFAR, X_GBACK, X_GRESID,
 X_GBACK2, X_GRES, X_PULL, X_OUT, X_COUNT) = range(31)


def lower_mask(ref, out, row0, col0, tile):
    rows, cols = ref.shape

    def body(i, c):
        at = pl.ds(pl.multiple_of(i * tile, tile), tile)
        row = row0 + i * tile + lax.broadcasted_iota(jnp.int32, (tile, cols), 0)
        col = col0 + lax.broadcasted_iota(jnp.int32, (tile, cols), 1)
        out[at, :] = jnp.where(row >= col, ref[at, :].astype(F32), 0.0).astype(BF16)
        return c

    lax.fori_loop(0, rows // tile, body, 0)


def dot(a, b):
    return jnp.dot(a, b, preferred_element_type=F32)


def dot_t(a, b):
    return lax.dot_general(a, b, (((0,), (0,)), ((), ())), preferred_element_type=F32)


def kernel(
    parent, tiles, sides, inverse_h, panels_h, tops, grand_h, child_h, root_h, cp_h, rg_h, rc_h,
    leaf_out, top_out,
    inverse, panels, grand, child, root, cp, rg, rc,
    in_sem, send_sem, recv_sem,
    sides_all, weight, solved_all, u0_out, u12_out, u0_in, u12_in,
    gright_out, gright, gred_out, gred, gsol, ctop_out, ctop, cred_out, cred, cright, cred2_out, cred2, csol,
    rred_out, rred, rright, rred2_out, rred2, rsol, rback_out, rback, rres, cback_out, cback, cresid,
    cback2_out, cback2, cres, cfar, gback_out, gback, gresid, gback2_out, gback2, gres,
    pulled, pull_out, pull, leafo_out, leafo, ancestor, rg_part, gb_part,
):
    l = lax.axis_index("leaf")
    p = lax.axis_index("panel")
    l8, l16 = l // 8 * 8, l // 16 * 16
    m8, m16 = l - l8, l - l16

    loads = []
    for i, (src, dst) in enumerate(
        [(inverse_h, inverse), (panels_h, panels), (grand_h, grand), (cp_h, cp), (rg_h, rg), (child_h, child), (rc_h, rc), (root_h, root)]
    ):
        copy = pltpu.make_async_copy(src, dst, in_sem.at[i])
        copy.start()
        loads.append(copy)

    barrier = pltpu.get_barrier_semaphore()

    def greet_leaf(k, c):
        pl.semaphore_signal(barrier, inc=1, device_id=(lax.rem(l + k, LEAF), p), device_id_type=MESH)
        return c

    def greet_panel(k, c):
        pl.semaphore_signal(barrier, inc=1, device_id=(l, lax.rem(p + k, PANEL)), device_id_type=MESH)
        return c

    lax.fori_loop(1, PANEL, greet_panel, 0)
    lax.fori_loop(1, LEAF, greet_leaf, 0)

    def send(x, src, dst, device):
        pltpu.make_async_remote_copy(src, dst, send_sem.at[x], recv_sem.at[x], device_id=device, device_id_type=MESH).start()

    def arrived(x, ref):
        pltpu.make_async_copy(ref, ref, recv_sem.at[x]).wait()

    def to_panel(x, src_of, dst):
        def body(k, c):
            q = lax.rem(p + k, PANEL)
            send(x, src_of(q), dst, (l, q))
            return c

        lax.fori_loop(1, PANEL, body, 0)

    def to_leaf(x, n, base, me, src_of, dst):
        def body(k, c):
            q = lax.rem(me + k, n)
            send(x, src_of(q), dst, (base + q, p))
            return c

        lax.fori_loop(n // 2, n, body, 0)
        lax.fori_loop(1, n // 2, body, 0)

    def total(ref):
        return jnp.sum(ref[...].astype(F32), axis=0)

    def flat(ref):
        return ref[...].reshape(ref.shape[0] * ref.shape[1], ref.shape[2])

    def scattered(value, out):
        out[...] = value.astype(BF16).reshape(out.shape)

    mine = parent[0]
    own_grand = [jnp.where(mine == g, 1.0, 0.0).astype(F32) for g in range(4)]
    own_child = [own_grand[0] + own_grand[1], own_grand[2] + own_grand[3]]
    slot = lax.broadcasted_iota(jnp.int32, (16, 128), 0)
    picks = jnp.zeros((16, 128), F32)
    for g in range(4):
        picks = picks + jnp.where(slot == g, own_grand[g], 0.0)
    for c in range(2):
        picks = picks + jnp.where(slot == 4 + c, own_child[c], 0.0)
    weight[l] = picks.astype(BF16)
    sides_all[p] = sides[...]

    pl.semaphore_wait(barrier, LEAF - 1 + PANEL - 1)

    to_panel(X_SIDES, lambda q: sides_all.at[p], sides_all.at[p])
    to_leaf(X_WEIGHT, LEAF, 0, l, lambda q: weight.at[l], weight.at[l])
    loads[0].wait()
    lower_mask(inverse, inverse, p * 256, 0, 32)
    arrived(X_SIDES, sides_all.at[pl.ds(0, PANEL - 1)])
    solved_all[p] = dot(inverse[...], flat(sides_all)).astype(BF16)
    to_panel(X_SOLVED, lambda q: solved_all.at[p], solved_all.at[p])
    loads[1].wait()
    loads[2].wait()
    lower_mask(grand, grand, m8 * 512, p * 512, 64)
    loads[5].wait()
    lower_mask(child, child, m16 * 256, p * 512, 64)
    loads[7].wait()
    lower_mask(root, root, l * 128, p * 512, 64)
    arrived(X_SOLVED, solved_all.at[pl.ds(0, PANEL - 1)])

    def update(k):
        for t in range(4):
            keep = tiles[0, k, p * 4 + t].astype(F32)
            value = dot(panels[k, t * 128:(t + 1) * 128, :], flat(solved_all)) * keep
            value = value.astype(BF16).reshape(8, 16, 128)
            if k == 0:
                u0_out[t * 8:(t + 1) * 8] = value
            else:
                u12_out[t * 8:(t + 1) * 8, (k - 1) * 16:k * 16] = value

    update(0)
    u0_in[l] = u0_out[l]
    to_leaf(X_U0, LEAF, 0, l, lambda q: u0_out.at[q], u0_in.at[l])
    update(1)
    update(2)
    u12_in[l] = u12_out[l]
    arrived(X_WEIGHT, weight.at[pl.ds(0, LEAF - 1)])
    arrived(X_U0, u0_in.at[pl.ds(0, LEAF - 1)])

    def collect(d, sums):
        w = weight[d].astype(F32)
        u = u0_in[d].astype(F32)
        return tuple(s - w[g:g + 1, :] * u for g, s in enumerate(sums))

    sums = lax.fori_loop(0, LEAF, collect, tuple(tops[g].astype(F32) for g in range(4)))
    for g in range(4):
        gright_out[g] = sums[g].astype(BF16)
    gright[l] = gright_out[l // 8]
    to_leaf(X_GRIGHT, LEAF, 0, l, lambda q: gright_out.at[q // 8], gright.at[l])
    to_leaf(X_U12, LEAF, 0, l, lambda q: u12_out.at[q], u12_in.at[l])
    arrived(X_GRIGHT, gright.at[pl.ds(0, LEAF - 1)])
    scattered(dot(grand[...], flat(gright)), gred_out)
    gred[p] = gred_out[p]
    to_panel(X_GRED, lambda q: gred_out.at[q], gred.at[p])
    arrived(X_U12, u12_in.at[pl.ds(0, LEAF - 1)])

    def collect12(d, sums):
        w = weight[d].astype(F32)
        u = u12_in[d].astype(F32)
        return (sums[0] - w[4:5, :] * u[0:16], sums[1] - w[5:6, :] * u[0:16], sums[2] - u[16:32])

    sums = lax.fori_loop(0, LEAF, collect12, tuple(tops[g].astype(F32) for g in range(4, 7)))
    ctop_out[0] = sums[0].astype(BF16)
    ctop_out[1] = sums[1].astype(BF16)
    root_top = sums[2]
    for c in range(2):
        owner = 16 * c + l // 2
        half = l - l // 2 * 2

        @pl.when(owner == l)
        def _():
            ctop[half] = ctop_out[c]

        @pl.when(owner != l)
        def _():
            send(X_CTOP, ctop_out.at[c], ctop.at[half], (owner, p))

    arrived(X_GRED, gred.at[pl.ds(0, PANEL - 1)])
    gsol[p] = total(gred).astype(BF16)
    to_panel(X_GSOL, lambda q: gsol.at[p], gsol.at[p])
    loads[3].wait()
    loads[4].wait()
    loads[6].wait()
    arrived(X_GSOL, gsol.at[pl.ds(0, PANEL - 1)])

    scattered(dot(cp[...], flat(gsol)), cred_out)
    cred[m16] = cred_out[m16]
    to_leaf(X_CRED, 16, l16, m16, lambda q: cred_out.at[q], cred.at[m16])
    rg_part[...] = dot(rg[...], flat(gsol))
    source_self = jnp.logical_or(l == 0, l == LEAF - 1)

    @pl.when(source_self)
    def _():
        arrived(X_CTOP, ctop.at[0])

    @pl.when(jnp.logical_not(source_self))
    def _():
        arrived(X_CTOP, ctop)

    arrived(X_CRED, cred.at[pl.ds(0, 15)])
    cright[m16] = (flat(ctop).astype(F32) - total(cred)).astype(BF16)
    to_leaf(X_CRIGHT, 16, l16, m16, lambda q: cright.at[m16], cright.at[m16])
    arrived(X_CRIGHT, cright.at[pl.ds(0, 15)])
    scattered(dot(child[...], flat(cright)), cred2_out)
    cred2[p] = cred2_out[p]
    to_panel(X_CRED2, lambda q: cred2_out.at[q], cred2.at[p])
    arrived(X_CRED2, cred2.at[pl.ds(0, PANEL - 1)])
    csol[p] = total(cred2).astype(BF16)
    to_panel(X_CSOL, lambda q: csol.at[p], csol.at[p])
    arrived(X_CSOL, csol.at[pl.ds(0, PANEL - 1)])

    scattered(dot(rc[...], flat(csol)) + rg_part[...], rred_out)
    rred[l] = rred_out[l]
    to_leaf(X_RRED, LEAF, 0, l, lambda q: rred_out.at[q], rred.at[l])
    arrived(X_RRED, rred.at[pl.ds(0, LEAF - 1)])
    rright[l] = (root_top - total(rred)).astype(BF16)
    to_leaf(X_RRIGHT, LEAF, 0, l, lambda q: rright.at[l], rright.at[l])
    arrived(X_RRIGHT, rright.at[pl.ds(0, LEAF - 1)])
    scattered(dot(root[...], flat(rright)), rred2_out)
    rred2[p] = rred2_out[p]
    to_panel(X_RRED2, lambda q: rred2_out.at[q], rred2.at[p])
    arrived(X_RRED2, rred2.at[pl.ds(0, PANEL - 1)])
    rsol[p] = total(rred2).astype(BF16)
    to_panel(X_RSOL, lambda q: rsol.at[p], rsol.at[p])
    arrived(X_RSOL, rsol.at[pl.ds(0, PANEL - 1)])
    scattered(dot_t(root[...], flat(rsol)), rback_out)
    rback[l] = rback_out[l]
    to_leaf(X_RBACK, LEAF, 0, l, lambda q: rback_out.at[q], rback.at[l])
    arrived(X_RBACK, rback.at[pl.ds(0, LEAF - 1)])
    rres[l] = total(rback).astype(BF16)
    top_out[6] = rres[l]
    to_leaf(X_RRES, LEAF, 0, l, lambda q: rres.at[l], rres.at[l])
    arrived(X_RRES, rres.at[pl.ds(0, LEAF - 1)])

    scattered(dot_t(rc[...], flat(rres)), cback_out)
    cback[p] = cback_out[p]
    to_panel(X_CBACK, lambda q: cback_out.at[q], cback.at[p])
    gb_part[...] = dot_t(rg[...], flat(rres))
    arrived(X_CBACK, cback.at[pl.ds(0, PANEL - 1)])
    cresid[p] = (csol[p].astype(F32) - total(cback)).astype(BF16)
    to_panel(X_CRESID, lambda q: cresid.at[p], cresid.at[p])

    def masked(k, value):
        for t in range(4):
            keep = tiles[0, k, p * 4 + t].astype(F32)
            ancestor[t * 128:(t + 1) * 128] = (value[t * 128:(t + 1) * 128] * keep).astype(BF16)

    def pull_from(k, first):
        for n in range(8):
            at = slice(n * 256, (n + 1) * 256)
            value = dot_t(panels[k, :, at], ancestor[...])
            pulled[at, :] = value if first else pulled[at, :] + value

    arrived(X_CRESID, cresid.at[pl.ds(0, PANEL - 1)])
    scattered(dot_t(child[...], flat(cresid)), cback2_out)
    cback2[m16] = cback2_out[m16]
    to_leaf(X_CBACK2, 16, l16, m16, lambda q: cback2_out.at[q], cback2.at[m16])
    masked(2, flat(rres).astype(F32))
    pull_from(2, True)
    arrived(X_CBACK2, cback2.at[pl.ds(0, 15)])
    cres[m16] = total(cback2).astype(BF16)
    to_leaf(X_CRES, 16, l16, m16, lambda q: cres.at[m16], cres.at[m16])

    def to_far(k, c):
        send(X_CFAR, cres.at[m16], cfar.at[m16], (16 - l16 + lax.rem(m16 + k, 16), p))
        return c

    lax.fori_loop(0, 16, to_far, 0)
    arrived(X_CRES, cres.at[pl.ds(0, 15)])

    scattered(dot_t(cp[...], flat(cres)) + gb_part[...], gback_out)
    gback[p] = gback_out[p]
    to_panel(X_GBACK, lambda q: gback_out.at[q], gback.at[p])
    arrived(X_GBACK, gback.at[pl.ds(0, PANEL - 1)])
    gresid[p] = (gsol[p].astype(F32) - total(gback)).astype(BF16)
    to_panel(X_GRESID, lambda q: gresid.at[p], gresid.at[p])
    arrived(X_GRESID, gresid.at[pl.ds(0, PANEL - 1)])
    scattered(dot_t(grand[...], flat(gresid)), gback2_out)
    gback2[m8] = gback2_out[m8]
    to_leaf(X_GBACK2, 8, l8, m8, lambda q: gback2_out.at[q], gback2.at[m8])
    arrived(X_CFAR, cfar)
    near = jnp.where(l < 16, 1.0, 0.0).astype(F32)
    from_near = own_child[0] * near + own_child[1] * (1.0 - near)
    masked(1, flat(cres).astype(F32) * from_near + flat(cfar).astype(F32) * (1.0 - from_near))
    pull_from(1, False)
    near16 = near.astype(F32)
    at16 = pl.ds(pl.multiple_of(lax.rem(l, 2) * 16, 16), 16)
    here = cres[l // 2, at16].astype(F32)
    there = cfar[l // 2, at16].astype(F32)
    top_out[4] = (here * near16 + there * (1.0 - near16)).astype(BF16)
    top_out[5] = (there * near16 + here * (1.0 - near16)).astype(BF16)
    arrived(X_GBACK2, gback2.at[pl.ds(0, 7)])
    gres[l] = total(gback2).astype(BF16)
    to_leaf(X_GRES, LEAF, 0, l, lambda q: gres.at[l], gres.at[l])
    arrived(X_GRES, gres.at[pl.ds(0, LEAF - 1)])

    def grand_of(g):
        return gres[g * 8:(g + 1) * 8].reshape(512, 128).astype(F32)

    masked(0, sum(grand_of(g) * own_grand[g] for g in range(4)))
    at64 = pl.ds(pl.multiple_of(lax.rem(l, 4) * 16, 16), 16)
    for g in range(4):
        top_out[g] = gres[g * 8 + l // 4, at64]
    for n in range(8):
        at = slice(n * 256, (n + 1) * 256)
        pull_out[n] = (pulled[at, :] + dot_t(panels[0, :, at], ancestor[...])).astype(BF16)
    pull[p] = pull_out[p]
    to_panel(X_PULL, lambda q: pull_out.at[q], pull.at[p])
    arrived(X_PULL, pull.at[pl.ds(0, PANEL - 1)])
    residual = (solved_all[p].astype(F32) - total(pull)).astype(BF16)
    for n in range(8):
        leafo_out[n] = dot_t(inverse[:, n * 256:(n + 1) * 256], residual).astype(BF16)
    leafo[p] = leafo_out[p]
    to_panel(X_OUT, lambda q: leafo_out.at[q], leafo.at[p])
    arrived(X_OUT, leafo.at[pl.ds(0, PANEL - 1)])
    leaf_out[...] = total(leafo).astype(BF16)

    def sent(x, ref):
        pltpu.make_async_copy(ref, ref, send_sem.at[x]).wait()

    for x, ref, n in [
        (X_SIDES, sides_all, 7), (X_WEIGHT, weight, 31), (X_SOLVED, solved_all, 7), (X_U0, u0_in, 31), (X_U12, u12_in, 31),
        (X_GRIGHT, gright, 31), (X_GRED, gred, 7), (X_GSOL, gsol, 7), (X_CRED, cred, 15), (X_CRIGHT, cright, 15),
        (X_CRED2, cred2, 7), (X_CSOL, csol, 7), (X_RRED, rred, 31), (X_RRIGHT, rright, 31), (X_RRED2, rred2, 7),
        (X_RSOL, rsol, 7), (X_RBACK, rback, 31), (X_RRES, rres, 31), (X_CBACK, cback, 7), (X_CRESID, cresid, 7),
        (X_CBACK2, cback2, 15), (X_CRES, cres, 15), (X_CFAR, cfar, 16), (X_GBACK, gback, 7), (X_GRESID, gresid, 7),
        (X_GBACK2, gback2, 7), (X_GRES, gres, 31), (X_PULL, pull, 7), (X_OUT, leafo, 7),
    ]:
        sent(x, ref.at[pl.ds(0, n)])

    @pl.when(source_self)
    def _():
        sent(X_CTOP, ctop.at[0])

    @pl.when(jnp.logical_not(source_self))
    def _():
        sent(X_CTOP, ctop)


def per_device(
    leaf_sides, leaf_inverse, leaf_panels, parent_map, tile_mask, top_sides,
    grand_inverse, child_inverse, root_inverse, child_panels, root_grand, root_child,
):
    def bf(*shape):
        return pltpu.VMEM(shape, BF16)

    def pieces(n, rows):
        return bf(n, rows, 128)

    vmem = pl.BlockSpec(memory_space=pltpu.VMEM)
    smem = pl.BlockSpec(memory_space=pltpu.SMEM)
    hbm = pl.BlockSpec(memory_space=pl.ANY)
    scratch = [
        bf(256, 2048), bf(3, 512, 2048), bf(512, 512), bf(256, 512), bf(128, 512), bf(512, 512), bf(512, 512), bf(512, 256),
        pltpu.SemaphoreType.DMA((8,)), pltpu.SemaphoreType.DMA((X_COUNT,)), pltpu.SemaphoreType.DMA((X_COUNT,)),
        pieces(8, 256), pieces(32, 16), pieces(8, 256), pieces(32, 16), pieces(32, 32), pieces(32, 16), pieces(32, 32),
        pieces(4, 16), pieces(32, 16), pieces(8, 64), pieces(8, 64), pieces(8, 64),
        pieces(2, 16), pieces(2, 16), pieces(16, 32), pieces(16, 32), pieces(16, 32),
        pieces(8, 32), pieces(8, 32), pieces(8, 32),
        pieces(32, 16), pieces(32, 16), pieces(32, 16),
        pieces(8, 16), pieces(8, 16), pieces(8, 16),
        pieces(32, 16), pieces(32, 16), pieces(32, 16),
        pieces(8, 32), pieces(8, 32), pieces(8, 32),
        pieces(16, 32), pieces(16, 32), pieces(16, 32), pieces(16, 32),
        pieces(8, 64), pieces(8, 64), pieces(8, 64),
        pieces(8, 64), pieces(8, 64), pieces(32, 64),
        pltpu.VMEM((2048, 128), F32), pieces(8, 256), pieces(8, 256), pieces(8, 256), pieces(8, 256),
        bf(512, 128), pltpu.VMEM((512, 128), F32), pltpu.VMEM((512, 128), F32),
    ]
    return pl.pallas_call(
        kernel,
        out_shape=(jax.ShapeDtypeStruct((256, 128), BF16), jax.ShapeDtypeStruct((7, 16, 128), BF16)),
        in_specs=[smem, smem, vmem, hbm, hbm, vmem, hbm, hbm, hbm, hbm, hbm, hbm],
        out_specs=(vmem, vmem),
        scratch_shapes=scratch,
        compiler_params=pltpu.CompilerParams(collective_id=0, has_side_effects=True, vmem_limit_bytes=40 << 20),
        cost_estimate=pl.CostEstimate(flops=2_400_000_000, bytes_accessed=12_000_000, transcendentals=0),
        name="solve",
    )(
        parent_map, tile_mask, leaf_sides, leaf_inverse, leaf_panels, top_sides,
        grand_inverse, child_inverse, root_inverse, child_panels, root_grand, root_child,
    )


def solution(mesh):
    placed = (
        P(("leaf", "panel"), None),
        P(("leaf", "panel"), None),
        P(None, "panel", "leaf"),
        P("leaf"),
        P("leaf", None, None),
        P(None, ("panel", "leaf"), None),
        P("leaf", "panel"),
        P("leaf", "panel"),
        P("leaf", "panel"),
        P("panel", "leaf"),
        P("panel", "leaf"),
        P("panel", "leaf"),
    )
    return jax.shard_map(
        per_device,
        mesh=mesh,
        in_specs=placed,
        out_specs=(P(("leaf", "panel"), None), P(None, ("panel", "leaf"), None)),
        check_vma=False,
    )
```

time: 1240 us -> 192 us (0.15)
  blocking collectives: 838 us -> 0 us
  waiting for transfers between devices: 342 us -> 0 us
  Pallas kernels: 0 us -> 176 us
  matrix products: 28.1 us -> 0 us
  between operations: 15.2 us -> 1.3 us
    psum x6 -> x0, blocking collectives: 731 us -> none  [level_total(): return lax.psum(partial_value, 'leaf').astype(jnp.bfloat16)]
    reduce_scatter x7 -> x0, waiting for transfers between devices: 342 us -> none  [reduce_rows(): lax.psum_scatter(partial_value, 'panel', scatter_dimension=0, tiled=True)]
    pallas_call x0 -> x1, Pallas kernels: none -> 176 us  [per_device(): pl.pallas_call(kernel, out_shape=(jax.ShapeDtypeStruct((256, 128), BF16),...]
    all_gather x7 -> x0, blocking collectives: 107 us -> none  [fold_rows(): lax.all_gather(portions, 'panel', axis=0, tiled=True)]
    dot_general x16 -> x0, matrix products: 28.1 us -> none  [the longest x7 8.1 us: transpose_product(): lax.dot_general(matrix, vectors, (((0,), (0,)), ((), ())), preferred_elem...]
    unnamed x28 -> x23, local copies, waits for them, and re-layouts: 0.15 us -> 13.4 us
  transfers between devices with their start and end apart: 7 -> 0, of which waited for: 7 -> 0; matrix products, arithmetic and copies ran while one was open for 0% -> 0% of each run, Pallas kernels for 0% -> 0%
where the time goes in v1:
time: 192 us; the launch traced here: 191 us
  Pallas kernels  176 us (92%)
  local copies, waits for them, and re-layouts  13.4 us (7%)
    pallas_call x1, Pallas kernels, per_device(): pl.pallas_call(kernel, out_shape=(jax.ShapeDtypeStruct((256, 128), BF16),...  176 us
    unnamed x23, local copies, waits for them, and re-layouts  13.4 us

profile of v1, /device:TPU:1, one launch (start us, length us, event | category | flops | bytes accessed | tf_op | source)
XLA Modules:
  0.0 191.2 jit_solution(17364096569427711136)
XLA Ops:
  1.3 0.7 copy.14.tiles
  2.0 0.0 copy-start
  2.0 2.8 %copy-done = bf16[3,512,2048]{2,1,0:T(8,128)(2,1)S(1)} copy-done((bf16[3,512,2048]{2,1,0:T(8,128)(2,1)S(1)}, bf16[3,512,2048]{2,1,0:T(8,128)(2,1)}, u32[]{:S(2)}) %copy-start) | copy-done | bytes 6291480
  4.7 0.0 copy-start.1
  4.7 1.2 copy-done.1
  6.0 0.0 copy-start.2
  6.0 1.0 copy-done.2
  7.0 0.0 copy-start.3
  7.0 1.0 copy-done.3
  8.1 0.0 copy-start.4
  8.1 1.0 copy-done.4
  9.1 0.0 copy-start.5
  9.1 0.9 copy-done.5
  10.0 0.0 copy-start.6
  10.0 0.9 copy-done.6
  11.0 0.0 copy-start.7
  11.0 0.9 copy-done.7
  11.9 0.0 copy-start.8
  11.9 0.8 copy-done.8
  12.7 0.0 copy-start.9
  12.7 0.7 copy-done.9
  13.5 176.4 %solve.1 = (bf16[256,128]{1,0:T(8,128)(2,1)S(1)}, bf16[7,16,128]{2,1,0:T(8,128)(2,1)S(1)}) custom-call(s32[1]{0:T(128)S(6)} %copy.17.parent, s32[1,3,32]{2,1,0:T(4,128)S(1)} %copy.14.tiles, bf16[256,128]{1,0:T(8,128)(2,1)S(1)} %copy-done.8, bf16[256,2048]{1,0:T(8,128)(2,1)S(1)} %copy-done.1, bf16[3,512,2048]{2,1,0:T(8,128)(2,1)S(1)} %copy-done, ...), custom_call_target="tpu_custom_call" | custom-call | flops 2400000000 | bytes 12000000 | tf_op jit(solution)/shard_map/solve/pallas_call | solution.py:390
  189.9 0.6 copy.18
  190.6 0.6 copy.19
Async XLA Ops:
  2.0 2.8 %copy-start = (bf16[3,512,2048]{2,1,0:T(8,128)(2,1)S(1)}, bf16[3,512,2048]{2,1,0:T(8,128)(2,1)}, u32[]{:S(2)}) copy-start(bf16[3,512,2048]{2,1,0:T(8,128)(2,1)} %panels_h.1) | copy-start | bytes 18874372
  4.7 1.2 copy-start.1
  6.0 1.0 copy-start.2
  7.0 1.0 copy-start.3
  8.1 1.0 copy-start.4
  9.1 0.9 copy-start.5
  10.0 0.9 copy-start.6
  11.0 0.9 copy-start.7
  11.9 0.8 copy-start.8
  12.7 0.7 copy-start.9

commit v2 on v1

v2 whole, which is shorter than its diff:
```python
import functools

import jax
import jax.numpy as jnp
from jax import lax
from jax.experimental import pallas as pl
from jax.experimental.pallas import tpu as pltpu
from jax.sharding import PartitionSpec as P

MESH = pl.DeviceIdType.MESH
F32 = jnp.float32
BF16 = jnp.bfloat16
LEAF = 32
PANEL = 8
VMEM_BYTES = 60 << 20

NAMES = (
    "SIDES", "SIDES_PAIR", "WEIGHT", "SOLVED", "SOLVED_PAIR", "U0", "GRIGHT", "GRED", "GSOL", "CHILD", "RC", "RLINE", "CTOP",
    "CRED", "CRIGHT", "CSIB", "RTOP", "RRED", "RRIGHT", "RSIB", "RBACK", "RRES", "RNAT", "CRSIB", "CBACK", "CRES", "CFAR",
    "GBACK", "GRESID", "GBACK2", "GRES", "PULL", "OUT",
)
X = {name: i for i, name in enumerate(NAMES)}


def lower_mask(ref, out, row0, col0, tile):
    rows, cols = ref.shape

    def body(i, c):
        at = pl.ds(pl.multiple_of(i * tile, tile), tile)
        row = row0 + i * tile + lax.broadcasted_iota(jnp.int32, (tile, cols), 0)
        col = col0 + lax.broadcasted_iota(jnp.int32, (tile, cols), 1)
        out[at, :] = jnp.where(row >= col, ref[at, :].astype(F32), 0.0).astype(BF16)
        return c

    lax.fori_loop(0, rows // tile, body, 0)


def dot(a, b):
    return jnp.dot(a, b, preferred_element_type=F32)


def dot_t(a, b):
    return lax.dot_general(a, b, (((0,), (0,)), ((), ())), preferred_element_type=F32)


def dot_nt(a, b):
    return lax.dot_general(a, b, (((1,), (1,)), ((), ())), preferred_element_type=F32)


def kernel(
    parent, tiles, sides_h, inverse_h, panels_h, tops_h, grand_h, child_h, root_h, cp_h, rg_h, rc_h,
    leaf_out, top_out,
    inverse, panels, grand, child_all, root, cp, rg, rc_all,
    in_sem, send_sem, recv_sem, pair_sem, z_sem, z_send_sem, round_sem,
    sides_all, tops, weight, solved_all, u0_out, u0_in, u1_part, u2_part, work,
    gright_out, gright, gred_out, gred, gsol, ctop_out, ctop, cred_out, cred, cpiece, cright, cs_out, cs_in, cs,
    rtop_out, rtop, rred_out, rred, rright, rs_out, rs_in, rs, rback_out, rback, rres, rnat, cr_out, cr_in,
    cback_out, cback, cres_piece, cnat, cfar, gback_out, gback, gresid, gback2_out, gback2, gres,
    pulled, pull_out, pull, leafo_out, leafo, ancestor, gb_part, inverse_t, panel_t, root_nat, child_nat, far_nat,
):
    l = lax.axis_index("leaf")
    p = lax.axis_index("panel")
    l8, l16 = l // 8 * 8, l // 16 * 16
    m8, m16 = l - l8, l - l16
    y = p // 2
    core = p - 2 * y
    own_y = m16 // 4
    own_i = m16 - 4 * own_y
    diag = own_y == y
    root_y = l // 8
    root_i = (l - 8 * root_y) // 2
    root_half = l - l // 2 * 2
    root_diag = root_y == y

    loads = []
    for i, (src, dst) in enumerate(
        [(inverse_h, inverse), (panels_h, panels), (grand_h, grand), (child_h, child_all.at[y]), (root_h, root.at[y]), (cp_h, cp), (rg_h, rg), (rc_h, rc_all.at[y]), (tops_h, tops), (sides_h, sides_all.at[p])]
    ):
        loads.append(pltpu.make_async_copy(src, dst, in_sem.at[i]))
    loads[9].start()
    loads[0].start()
    loads[8].start()

    barrier = pltpu.get_barrier_semaphore()

    x_of = lax.rem(l, 4)
    x_peers = [l - x_of + lax.rem(x_of + k, 4) for k in range(1, 4)]
    z_peers = {k: lax.rem(l + 4 * k, LEAF) for k in range(1, 8)}

    def signal(semaphore, leaf, panel):
        pl.semaphore_signal(semaphore, inc=1, device_id=(leaf, panel), device_id_type=MESH)

    for k in range(1, PANEL):
        signal(barrier, l, lax.rem(p + k, PANEL))
    for there in x_peers + [z_peers[1], z_peers[7]]:
        signal(barrier, there, p)

    def send(x, src, dst, device):
        pltpu.make_async_remote_copy(src, dst, send_sem.at[X[x]], recv_sem.at[X[x]], device_id=device, device_id_type=MESH).start()

    def arrived(x, ref):
        pltpu.make_async_copy(ref, ref, recv_sem.at[X[x]]).wait()

    def to_panel(x, src_of, dst):
        def body(k, c):
            q = lax.rem(p + k, PANEL)
            send(x, src_of(q), dst, (l, q))
            return c

        lax.fori_loop(1, PANEL, body, 0)

    def to_leaf(x, n, base, me, src_of, dst):
        def body(k, c):
            q = lax.rem(me + k, n)
            send(x, src_of(q), dst, (base + q, p))
            return c

        lax.fori_loop(n // 2, n, body, 0)
        lax.fori_loop(1, n // 2, body, 0)

    def total(ref):
        return jnp.sum(ref[...].astype(F32), axis=0)

    def flat(ref):
        return ref[...].reshape(ref.shape[0] * ref.shape[1], ref.shape[2])

    def scattered(value, out):
        out[...] = value.astype(BF16).reshape(out.shape)

    def arrived_but_self(x, ref, has_self, n):
        @pl.when(has_self)
        def _():
            arrived(x, ref.at[pl.ds(0, n - 1)])

        @pl.when(jnp.logical_not(has_self))
        def _():
            arrived(x, ref.at[pl.ds(0, n)])

    def to_line(x, n, base, me, src, dst, q):
        def body(k, c):
            there = base + lax.rem(me + k, n)

            @pl.when(jnp.logical_or(there != l, q != p))
            def _():
                send(x, src, dst, (there, q))

            return c

        lax.fori_loop(n // 2, n, body, 0)
        lax.fori_loop(0, n // 2, body, 0)

    def to_sibling(x, src, dst):
        send(x, src, dst, (l, p + 1 - 2 * core))

    def to_chips(x, src, dst):
        def body(k, c):
            send(x, src, dst, (l, lax.rem(p + 2 * k, PANEL)))
            return c

        lax.fori_loop(1, 4, body, 0)

    def gather_panel(which, x, ref, beside):
        to_chips_each(which, x, ref)
        to_sibling(x + "_PAIR", ref.at[p], ref.at[p])
        beside()
        for k in range(1, 4):
            came = lax.rem(p + PANEL - 2 * k, PANEL)
            pltpu.make_async_copy(ref.at[came], ref.at[came], pair_sem.at[which, k]).wait()
            to_sibling(x + "_PAIR", ref.at[came], ref.at[came])
        arrived(x + "_PAIR", ref.at[pl.ds(0, 4)])

    def to_chips_each(which, x, ref):
        for k in range(1, 4):
            pltpu.make_async_remote_copy(
                ref.at[p], ref.at[p], send_sem.at[X[x]], pair_sem.at[which, k],
                device_id=(l, lax.rem(p + 2 * k, PANEL)), device_id_type=MESH,
            ).start()

    def cut(value, store):
        value = value.astype(BF16)
        for j in range(4):
            for i in range(4):
                store(4 * j + i, value[32 * j:32 * j + 32, 128 * i:128 * i + 128])

    def strip(ref, j):
        return jnp.concatenate([ref[4 * j + i] for i in range(4)], axis=1)

    def put_strip(ref, j, value):
        value = value.astype(BF16)
        for i in range(4):
            ref[4 * j + i] = value[:, 128 * i:128 * i + 128]

    def strip2(ref, j):
        return jnp.concatenate(
            [jnp.concatenate([ref[8 * j + 2 * i], ref[8 * j + 2 * i + 1]], axis=0) for i in range(4)], axis=1
        )

    def put_strip2(ref, j, value):
        value = value.astype(BF16)
        for i in range(4):
            for h in range(2):
                ref[8 * j + 2 * i + h] = value[16 * h:16 * h + 16, 128 * i:128 * i + 128]

    def natural(src, dst):
        n = src.shape[0] // 4
        for i in range(4):
            block = jnp.concatenate([src[n * i + j] for j in range(n)], axis=0).astype(F32)
            dst[128 * i:128 * i + 128] = block.T.astype(BF16)

    mine = parent[0]
    own_grand = [jnp.where(mine == g, 1.0, 0.0).astype(F32) for g in range(4)]
    own_child = [own_grand[0] + own_grand[1], own_grand[2] + own_grand[3]]
    slot = lax.broadcasted_iota(jnp.int32, (16, 128), 0)
    picks = jnp.zeros((16, 128), F32)
    for g in range(4):
        picks = picks + jnp.where(slot == g, own_grand[g], 0.0)
    weight[l] = picks.astype(BF16)
    share = pl.ds(pl.multiple_of(l * 16, 16), 16)

    pl.semaphore_wait(barrier, PANEL - 1 + 5)
    loads[9].wait()

    def first_rounds():
        for there in (z_peers[1], z_peers[7]):
            signal(round_sem.at[0], there, p)
        loads[1].start()
        loads[0].wait()
        lower_mask(inverse, inverse, p * 256, 0, 32)
        pl.semaphore_wait(round_sem.at[0], 2)
        for there in (z_peers[2], z_peers[6]):
            signal(round_sem.at[1], there, p)

    gather_panel(0, "SIDES", sides_all, first_rounds)
    solved_all[p] = dot(inverse[...], flat(sides_all)).astype(BF16)

    def last_round():
        pl.semaphore_wait(round_sem.at[1], 2)
        for there in x_peers:
            signal(round_sem.at[2], there, p)
        for copy in loads[2:8]:
            copy.start()
        loads[1].wait()
        loads[2].wait()
        lower_mask(grand, grand, m8 * 512, p * 512, 64)

    gather_panel(1, "SOLVED", solved_all, last_round)
    pl.semaphore_wait(round_sem.at[2], 3)

    loads[8].wait()

    def update(k, t):
        keep = tiles[0, k, p * 4 + t].astype(F32)
        return dot(panels[k, t * 128:(t + 1) * 128, :], flat(solved_all)) * keep

    for t in range(4):
        u0_out[t * 8:(t + 1) * 8] = update(0, t).astype(BF16).reshape(8, 16, 128)
    u0_in[l] = u0_out[l]
    to_leaf("U0", LEAF, 0, l, lambda q: u0_out.at[q], u0_in.at[l])
    to_leaf("WEIGHT", LEAF, 0, l, lambda q: weight.at[l], weight.at[l])
    loads[3].wait()
    lower_mask(child_all.at[y], child_all.at[y], m16 * 256, p * 512, 64)
    loads[4].wait()
    lower_mask(root.at[y], root.at[y], l * 128, p * 512, 64)
    to_chips("CHILD", child_all.at[y], child_all.at[y])

    to_chips("RLINE", root.at[y], root.at[y])
    for t in range(4):
        at = slice(t * 128, (t + 1) * 128)
        u1_part[at] = update(1, t)
        u2_part[at] = update(2, t)
    u2_part[share] = u2_part[share] - tops[6].astype(F32)
    for c in range(2):
        work[...] = u1_part[...] * own_child[c]
        work[share] = work[share] - tops[4 + c].astype(F32)

        def store(j, v):
            ctop_out[16 * c + j] = v

        cut(work[...].T, store)
    ctop[l] = ctop_out[l]
    arrived("WEIGHT", weight.at[pl.ds(0, LEAF - 1)])
    arrived("U0", u0_in.at[pl.ds(0, LEAF - 1)])

    def collect(d, sums):
        w = weight[d].astype(F32)
        u = u0_in[d].astype(F32)
        return tuple(s - w[g:g + 1, :] * u for g, s in enumerate(sums))

    sums = lax.fori_loop(0, LEAF, collect, tuple(tops[g].astype(F32) for g in range(4)), unroll=4)
    for g in range(4):
        gright_out[g] = sums[g].astype(BF16)
    gright[l] = gright_out[l // 8]
    to_leaf("GRIGHT", LEAF, 0, l, lambda q: gright_out.at[q // 8], gright.at[l])
    to_leaf("CTOP", LEAF, 0, l, lambda q: ctop_out.at[q], ctop.at[l])
    arrived("GRIGHT", gright.at[pl.ds(0, LEAF - 1)])
    scattered(dot(grand[...], flat(gright)), gred_out)
    gred[p] = gred_out[p]
    to_panel("GRED", lambda q: gred_out.at[q], gred.at[p])
    arrived("CTOP", ctop.at[pl.ds(0, LEAF - 1)])
    cpiece[...] = total(ctop)
    arrived("GRED", gred.at[pl.ds(0, PANEL - 1)])
    gsol[p] = total(gred).astype(BF16)
    to_panel("GSOL", lambda q: gsol.at[p], gsol.at[p])
    for i in range(5, 8):
        loads[i].wait()
    arrived("GSOL", gsol.at[pl.ds(0, PANEL - 1)])

    def store(j, v):
        cred_out[j] = v

    cut(dot(cp[...], flat(gsol)).T, store)
    cred[m16] = cred_out[m16]
    to_leaf("CRED", 16, l16, m16, lambda q: cred_out.at[q], cred.at[m16])
    to_chips("RC", rc_all.at[y], rc_all.at[y])

    back = (dot(rg[...], flat(gsol)) + u2_part[...]).T.astype(BF16)
    for j in range(4):
        for i in range(4):
            for h in range(2):
                at = 32 * j + 16 * h
                rtop_out[8 * j + 2 * i + h] = back[at:at + 16, 128 * i:128 * i + 128]

    arrived("CRED", cred.at[pl.ds(0, 15)])
    cres_piece[0] = (-(cpiece[...] + total(cred))).astype(BF16)
    to_line("CRIGHT", 16, l16, m16, cres_piece.at[0], cright.at[4 * y + own_i], 2 * own_y + core)

    @pl.when(diag)
    def _():
        cright[4 * y + own_i] = cres_piece[0]

    def to_rtop(k, c):
        j = lax.rem(k, 4)
        there = 8 * y + k // 4
        q = 2 * j + core

        @pl.when(jnp.logical_or(there != l, q != p))
        def _():
            send("RTOP", rtop_out.at[8 * j + k // 4], rtop.at[l], (there, q))

        return c

    lax.fori_loop(0, 32, to_rtop, 0)

    @pl.when(root_diag)
    def _():
        rtop[l] = rtop_out[l]

    arrived("CHILD", child_all.at[pl.ds(0, 3)])
    arrived_but_self("CRIGHT", cright, diag, 16)

    def summed(x, value, out, inbox):
        out[...] = value.astype(BF16)
        to_sibling(x, out, inbox)
        arrived(x, inbox)
        return out[...].astype(F32) + inbox[...].astype(F32)

    cs[...] = summed("CSIB", sum(dot_nt(strip(cright, j), child_all[j]) for j in range(4)), cs_out, cs_in).astype(BF16)
    arrived("RC", rc_all.at[pl.ds(0, 3)])

    for j in range(4):
        put_strip2(rred_out, j, dot_nt(cs[...], rc_all[j]))
    rred[l] = rred_out[l]
    to_leaf("RRED", LEAF, 0, l, lambda q: rred_out.at[q], rred.at[l])
    for n in range(8):
        at = slice(n * 256, (n + 1) * 256)
        inverse_t[at, :] = inverse[:, at].T
    arrived_but_self("RTOP", rtop, root_diag, 32)
    root_top = total(rtop)
    arrived("RLINE", root.at[pl.ds(0, 3)])
    arrived("RRED", rred.at[pl.ds(0, LEAF - 1)])
    rright[l] = (-(root_top + total(rred))).astype(BF16)
    to_leaf("RRIGHT", LEAF, 0, l, lambda q: rright.at[l], rright.at[l])
    for n in range(8):
        at = slice(n * 256, (n + 1) * 256)
        panel_t[at, :] = panels[0, :, at].T
    arrived("RRIGHT", rright.at[pl.ds(0, LEAF - 1)])
    rs[...] = summed("RSIB", sum(dot_nt(strip2(rright, j), root[j]) for j in range(4)), rs_out, rs_in).astype(BF16)
    for j in range(4):
        put_strip2(rback_out, j, dot(rs[...], root[j]))
    rback[l] = rback_out[l]
    to_leaf("RBACK", LEAF, 0, l, lambda q: rback_out.at[q], rback.at[l])
    arrived("RBACK", rback.at[pl.ds(0, LEAF - 1)])
    rres[l] = total(rback).astype(BF16)
    to_leaf("RRES", LEAF, 0, l, lambda q: rres.at[l], rres.at[l])
    rnat_at = 8 * root_i + 2 * y + root_half
    to_line("RNAT", LEAF, 0, l, rres.at[l], rnat.at[rnat_at], 2 * root_y + core)

    @pl.when(root_diag)
    def _():
        rnat[rnat_at] = rres[l]

    arrived("RRES", rres.at[pl.ds(0, LEAF - 1)])

    crs = summed("CRSIB", sum(dot(strip2(rres, j), rc_all[j]) for j in range(4)), cr_out, cr_in)
    residual_c = (cs[...].astype(F32) - crs).astype(BF16)
    for j in range(4):
        put_strip(cback_out, j, dot(residual_c, child_all[j]))
    cback[m16] = cback_out[m16]
    to_leaf("CBACK", 16, l16, m16, lambda q: cback_out.at[q], cback.at[m16])

    def masked(k, value):
        for t in range(4):
            keep = tiles[0, k, p * 4 + t].astype(F32)
            ancestor[t * 128:(t + 1) * 128] = (value[t * 128:(t + 1) * 128] * keep).astype(BF16)

    def pull_from(k, first):
        for n in range(8):
            at = slice(n * 256, (n + 1) * 256)
            value = dot_t(panels[k, :, at], ancestor[...])
            pulled[at, :] = value if first else pulled[at, :] + value

    arrived_but_self("RNAT", rnat, root_diag, 32)
    natural(rnat, root_nat)
    gb_part[...] = dot_t(rg[...], root_nat[...])
    arrived("CBACK", cback.at[pl.ds(0, 15)])
    cres_piece[1] = total(cback).astype(BF16)
    to_line("CRES", 16, l16, m16, cres_piece.at[1], cnat.at[4 * own_i + y], 2 * own_y + core)
    to_line("CFAR", 16, 16 - l16, m16, cres_piece.at[1], cfar.at[4 * own_i + y], 2 * own_y + core)

    @pl.when(diag)
    def _():
        cnat[4 * own_i + y] = cres_piece[1]

    top_out[6] = root_nat[share]
    masked(2, root_nat[...].astype(F32))
    pull_from(2, True)
    arrived_but_self("CRES", cnat, diag, 16)
    natural(cnat, child_nat)

    scattered(dot_t(cp[...], child_nat[...]) + gb_part[...], gback_out)
    gback[p] = gback_out[p]
    to_panel("GBACK", lambda q: gback_out.at[q], gback.at[p])
    arrived("CFAR", cfar)
    natural(cfar, far_nat)
    arrived("GBACK", gback.at[pl.ds(0, PANEL - 1)])
    gresid[p] = (gsol[p].astype(F32) - total(gback)).astype(BF16)
    to_panel("GRESID", lambda q: gresid.at[p], gresid.at[p])
    near = jnp.where(l < 16, 1.0, 0.0).astype(F32)
    here = child_nat[share].astype(F32)
    there = far_nat[share].astype(F32)
    top_out[4] = (here * near + there * (1.0 - near)).astype(BF16)
    top_out[5] = (there * near + here * (1.0 - near)).astype(BF16)
    from_near = own_child[0] * near + own_child[1] * (1.0 - near)
    masked(1, child_nat[...].astype(F32) * from_near + far_nat[...].astype(F32) * (1.0 - from_near))
    arrived("GRESID", gresid.at[pl.ds(0, PANEL - 1)])
    scattered(dot_t(grand[...], flat(gresid)), gback2_out)
    gback2[m8] = gback2_out[m8]
    to_leaf("GBACK2", 8, l8, m8, lambda q: gback2_out.at[q], gback2.at[m8])
    pull_from(1, False)
    arrived("GBACK2", gback2.at[pl.ds(0, 7)])
    gres[l] = total(gback2).astype(BF16)
    order = (4, 3, 5, 2, 6, 1, 7)
    for k in order:
        pltpu.make_async_remote_copy(
            gres.at[l], gres.at[l], z_send_sem, z_sem.at[k], device_id=(z_peers[k], p), device_id_type=MESH
        ).start()
    for there in x_peers:
        send("GRES", gres.at[l], gres.at[l], (there, p))
    for k in order[::-1]:
        came = z_peers[8 - k]
        pltpu.make_async_copy(gres.at[came], gres.at[came], z_sem.at[k]).wait()
        for there in x_peers:
            send("GRES", gres.at[came], gres.at[came], (there, p))
    arrived("GRES", gres.at[pl.ds(0, 24)])

    def grand_of(g):
        return gres[g * 8:(g + 1) * 8].reshape(512, 128).astype(F32)

    masked(0, sum(grand_of(g) * own_grand[g] for g in range(4)))
    at64 = pl.ds(pl.multiple_of(lax.rem(l, 4) * 16, 16), 16)
    for n in range(8):
        at = slice(n * 256, (n + 1) * 256)
        pull_out[n] = (pulled[at, :] + dot(panel_t[at, :], ancestor[...])).astype(BF16)
    pull[p] = pull_out[p]
    to_panel("PULL", lambda q: pull_out.at[q], pull.at[p])
    for g in range(4):
        top_out[g] = gres[g * 8 + l // 4, at64]
    arrived("PULL", pull.at[pl.ds(0, PANEL - 1)])
    residual = (solved_all[p].astype(F32) - total(pull)).astype(BF16)
    for n in range(8):
        leafo_out[n] = dot(inverse_t[n * 256:(n + 1) * 256, :], residual).astype(BF16)
    leafo[p] = leafo_out[p]
    to_panel("OUT", lambda q: leafo_out.at[q], leafo.at[p])
    arrived("OUT", leafo.at[pl.ds(0, PANEL - 1)])
    leaf_out[...] = total(leafo).astype(BF16)

    def sent(x, ref):
        pltpu.make_async_copy(ref, ref, send_sem.at[X[x]]).wait()

    for x, ref, n in [
        ("SIDES", sides_all, 3), ("SIDES_PAIR", sides_all, 4), ("SOLVED_PAIR", solved_all, 4), ("WEIGHT", weight, 31), ("SOLVED", solved_all, 3), ("U0", u0_in, 31), ("GRIGHT", gright, 31),
        ("GRED", gred, 7), ("GSOL", gsol, 7), ("CHILD", child_all, 3), ("RC", rc_all, 3), ("RLINE", root, 3), ("CTOP", ctop, 31), ("CRED", cred, 15),
        ("RRED", rred, 31), ("RRIGHT", rright, 31), ("RBACK", rback, 31), ("RRES", rres, 31), ("CBACK", cback, 15),
        ("CFAR", cfar, 16), ("GBACK", gback, 7), ("GRESID", gresid, 7), ("GBACK2", gback2, 7), ("GRES", gres, 24),
        ("PULL", pull, 7), ("OUT", leafo, 7),
    ]:
        sent(x, ref.at[pl.ds(0, n)])
    pltpu.make_async_copy(gres.at[pl.ds(0, 7)], gres.at[pl.ds(0, 7)], z_send_sem).wait()
    for x, ref in [("CSIB", cs_in), ("RSIB", rs_in), ("CRSIB", cr_in)]:
        sent(x, ref)

    @pl.when(diag)
    def _():
        for x, ref, n in [("CRIGHT", cright, 15), ("CRES", cnat, 15)]:
            sent(x, ref.at[pl.ds(0, n)])

    @pl.when(jnp.logical_not(diag))
    def _():
        for x, ref in [("CRIGHT", cright), ("CRES", cnat)]:
            sent(x, ref)

    @pl.when(root_diag)
    def _():
        for x, ref in [("RTOP", rtop), ("RNAT", rnat)]:
            sent(x, ref.at[pl.ds(0, 31)])

    @pl.when(jnp.logical_not(root_diag))
    def _():
        for x, ref in [("RTOP", rtop), ("RNAT", rnat)]:
            sent(x, ref)


def per_device(
    leaf_sides, leaf_inverse, leaf_panels, parent_map, tile_mask, top_sides,
    grand_inverse, child_inverse, root_inverse, child_panels, root_grand, root_child,
):
    def bf(*shape):
        return pltpu.VMEM(shape, BF16)

    def pieces(n, rows):
        return bf(n, rows, 128)

    vmem = pl.BlockSpec(memory_space=pltpu.VMEM)
    smem = pl.BlockSpec(memory_space=pltpu.SMEM)
    hbm = pl.BlockSpec(memory_space=pltpu.HBM)
    def f32(*shape):
        return pltpu.VMEM(shape, F32)

    sems = pltpu.SemaphoreType.DMA((len(X),))
    scratch = [
        bf(256, 2048), bf(3, 512, 2048), bf(512, 512), bf(4, 256, 512), bf(4, 128, 512),
        bf(512, 512), bf(512, 512), bf(4, 512, 256), pltpu.SemaphoreType.DMA((10,)), sems, sems,
        pltpu.SemaphoreType.DMA((2, 4)), pltpu.SemaphoreType.DMA((8,)), pltpu.SemaphoreType.DMA, pltpu.SemaphoreType.REGULAR((3,)),
        pieces(8, 256), bf(7, 16, 128), pieces(32, 16), pieces(8, 256), pieces(32, 16), pieces(32, 16),
        f32(512, 128), f32(512, 128), f32(512, 128),
        pieces(4, 16), pieces(32, 16), pieces(8, 64), pieces(8, 64), pieces(8, 64),
        pieces(32, 32), pieces(32, 32), pieces(16, 32), pieces(16, 32),
        f32(32, 128), pieces(16, 32), bf(32, 256), bf(32, 256), bf(32, 256),
        pieces(32, 16), pieces(32, 16), pieces(32, 16), pieces(32, 16), pieces(32, 16),
        bf(32, 128), bf(32, 128), bf(32, 128), pieces(32, 16), pieces(32, 16), pieces(32, 16),
        pieces(32, 16), bf(32, 256), bf(32, 256),
        pieces(16, 32), pieces(16, 32), pieces(2, 32), pieces(16, 32), pieces(16, 32),
        pieces(8, 64), pieces(8, 64), pieces(8, 64),
        pieces(8, 64), pieces(8, 64), pieces(32, 64),
        f32(2048, 128), pieces(8, 256), pieces(8, 256), pieces(8, 256), pieces(8, 256),
        bf(512, 128), f32(512, 128), bf(2048, 256), bf(2048, 512), bf(512, 128), bf(512, 128), bf(512, 128),
    ]
    return pl.pallas_call(
        kernel,
        out_shape=(jax.ShapeDtypeStruct((256, 128), BF16), jax.ShapeDtypeStruct((7, 16, 128), BF16)),
        in_specs=[smem, smem, hbm, hbm, hbm, hbm, hbm, hbm, hbm, hbm, hbm, hbm],
        out_specs=(vmem, vmem),
        scratch_shapes=scratch,
        compiler_params=pltpu.CompilerParams(collective_id=0, has_side_effects=True, vmem_limit_bytes=VMEM_BYTES),
        cost_estimate=pl.CostEstimate(flops=2_400_000_000, bytes_accessed=12_000_000, transcendentals=0),
        name="solve",
    )(
        parent_map, tile_mask, leaf_sides, leaf_inverse, leaf_panels, top_sides,
        grand_inverse, child_inverse, root_inverse, child_panels, root_grand, root_child,
    )


def solution(mesh):
    placed = (
        P(("leaf", "panel"), None),
        P(("leaf", "panel"), None),
        P(None, "panel", "leaf"),
        P("leaf"),
        P("leaf", None, None),
        P(None, ("panel", "leaf"), None),
        P("leaf", "panel"),
        P("leaf", "panel"),
        P("leaf", "panel"),
        P("panel", "leaf"),
        P("panel", "leaf"),
        P("panel", "leaf"),
    )
    return jax.shard_map(
        per_device,
        mesh=mesh,
        in_specs=placed,
        out_specs=(P(("leaf", "panel"), None), P(None, ("panel", "leaf"), None)),
        check_vma=False,
    )
```

time: 192 us -> 168 us (0.88)
  Pallas kernels: 176 us -> 162 us
  local copies, waits for them, and re-layouts: 13.4 us -> 4.09 us
    pallas_call x1, Pallas kernels: 176 us -> 162 us  [per_device(): pl.pallas_call(kernel, out_shape=(jax.ShapeDtypeStruct((256, 128), BF16),...]
    unnamed x23 -> x3, local copies, waits for them, and re-layouts: 13.4 us -> 4.09 us
where the time goes in v2:
time: 168 us
  Pallas kernels  162 us (96%)
  local copies, waits for them, and re-layouts  4.09 us (2%)
    pallas_call x1, Pallas kernels, per_device(): pl.pallas_call(kernel, out_shape=(jax.ShapeDtypeStruct((256, 128), BF16),...  162 us
    unnamed x3, local copies, waits for them, and re-layouts  4.09 us

profile of v2, /device:TPU:1, one launch (start us, length us, event | category | flops | bytes accessed | tf_op | source)
XLA Modules:
  0.0 167.6 jit_solution(790856128123395350)
XLA Ops:
  1.3 1.3 copy.14.tiles
  2.5 162.3 %solve.1 = (bf16[256,128]{1,0:T(8,128)(2,1)}, bf16[7,16,128]{2,1,0:T(8,128)(2,1)}) custom-call(s32[1]{0:T(128)S(6)} %copy.17.parent, s32[1,3,32]{2,1,0:T(4,128)} %copy.14.tiles, bf16[256,128]{1,0:T(8,128)(2,1)} %sides_h.1, bf16[256,2048]{1,0:T(8,128)(2,1)} %inverse_h.1, bf16[3,512,2048]{2,1,0:T(8,128)(2,1)} %panels_h.1, bf16[7,16,128]{2,1,0:T(8,128)(2,1)} %tops_h.1, ...), custom_call_target="tpu_custom_call" | custom-call | flops 2400000000 | bytes 12000000 | tf_op jit(solution)/shard_map/solve/pallas_call | solution.py:558
  164.8 1.5 copy.18
  166.3 1.4 copy.19

commit v3 on v2

--- a/solution.py
+++ b/solution.py
@@ -48,11 +48,11 @@
 
 
 def kernel(
-    parent, tiles, sides_h, inverse_h, panels_h, tops_h, grand_h, child_h, root_h, cp_h, rg_h, rc_h,
+    parent, tiles_h, sides_h, inverse_h, panels_h, tops_h, grand_h, child_h, root_h, cp_h, rg_h, rc_h,
     leaf_out, top_out,
     inverse, panels, grand, child_all, root, cp, rg, rc_all,
     in_sem, send_sem, recv_sem, pair_sem, z_sem, z_send_sem, round_sem,
-    sides_all, tops, weight, solved_all, u0_out, u0_in, u1_part, u2_part, work,
+    sides_all, tops, tiles, weight, solved_all, u0_out, u0_in, u1_part, u2_part, work,
     gright_out, gright, gred_out, gred, gsol, ctop_out, ctop, cred_out, cred, cpiece, cright, cs_out, cs_in, cs,
     rtop_out, rtop, rred_out, rred, rright, rs_out, rs_in, rs, rback_out, rback, rres, rnat, cr_out, cr_in,
     cback_out, cback, cres_piece, cnat, cfar, gback_out, gback, gresid, gback2_out, gback2, gres,
@@ -74,12 +74,13 @@
 
     loads = []
     for i, (src, dst) in enumerate(
-        [(inverse_h, inverse), (panels_h, panels), (grand_h, grand), (child_h, child_all.at[y]), (root_h, root.at[y]), (cp_h, cp), (rg_h, rg), (rc_h, rc_all.at[y]), (tops_h, tops), (sides_h, sides_all.at[p])]
+        [(inverse_h, inverse), (panels_h, panels), (grand_h, grand), (child_h, child_all.at[y]), (root_h, root.at[y]), (cp_h, cp), (rg_h, rg), (rc_h, rc_all.at[y]), (tops_h, tops), (sides_h, sides_all.at[p]), (tiles_h, tiles)]
     ):
         loads.append(pltpu.make_async_copy(src, dst, in_sem.at[i]))
     loads[9].start()
     loads[0].start()
     loads[8].start()
+    loads[10].start()
 
     barrier = pltpu.get_barrier_semaphore()
 
@@ -247,15 +248,30 @@
     pl.semaphore_wait(round_sem.at[2], 3)
 
     loads[8].wait()
+    loads[10].wait()
 
     def update(k, t):
-        keep = tiles[0, k, p * 4 + t].astype(F32)
+        keep = tiles[k, 0, p * 4 + t].astype(F32)
         return dot(panels[k, t * 128:(t + 1) * 128, :], flat(solved_all)) * keep
 
-    for t in range(4):
-        u0_out[t * 8:(t + 1) * 8] = update(0, t).astype(BF16).reshape(8, 16, 128)
+    for step in range(4):
+        t = lax.rem(l // 8 + 1 + step, 4)
+        keep = tiles[0, 0, p * 4 + t].astype(F32)
+        rows = pl.ds(pl.multiple_of(t * 128, 128), 128)
+        value = dot(panels[0, rows, :], flat(solved_all)) * keep
+        u0_out[pl.ds(t * 8, 8)] = value.astype(BF16).reshape(8, 16, 128)
+
+        def give(k, c):
+            there = t * 8 + lax.rem(m8 + k, 8)
+
+            @pl.when(there != l)
+            def _():
+                send("U0", u0_out.at[there], u0_in.at[l], (there, p))
+
+            return c
+
+        lax.fori_loop(0, 8, give, 0)
     u0_in[l] = u0_out[l]
-    to_leaf("U0", LEAF, 0, l, lambda q: u0_out.at[q], u0_in.at[l])
     to_leaf("WEIGHT", LEAF, 0, l, lambda q: weight.at[l], weight.at[l])
     loads[3].wait()
     lower_mask(child_all.at[y], child_all.at[y], m16 * 256, p * 512, 64)
@@ -400,7 +416,7 @@
 
     def masked(k, value):
         for t in range(4):
-            keep = tiles[0, k, p * 4 + t].astype(F32)
+            keep = tiles[k, 0, p * 4 + t].astype(F32)
             ancestor[t * 128:(t + 1) * 128] = (value[t * 128:(t + 1) * 128] * keep).astype(BF16)
 
     def pull_from(k, first):
@@ -468,19 +484,25 @@
 
     masked(0, sum(grand_of(g) * own_grand[g] for g in range(4)))
     at64 = pl.ds(pl.multiple_of(lax.rem(l, 4) * 16, 16), 16)
-    for n in range(8):
-        at = slice(n * 256, (n + 1) * 256)
-        pull_out[n] = (pulled[at, :] + dot(panel_t[at, :], ancestor[...])).astype(BF16)
+    panel_order = (4, 5, 3, 2, 6, 7, 1, 0)
+    for k in panel_order:
+        q = lax.rem(p + k, PANEL)
+        rows = pl.ds(pl.multiple_of(q * 256, 256), 256)
+        pull_out[q] = (pulled[rows, :] + dot(panel_t[rows, :], ancestor[...])).astype(BF16)
+        if k:
+            send("PULL", pull_out.at[q], pull.at[p], (l, q))
     pull[p] = pull_out[p]
-    to_panel("PULL", lambda q: pull_out.at[q], pull.at[p])
     for g in range(4):
         top_out[g] = gres[g * 8 + l // 4, at64]
     arrived("PULL", pull.at[pl.ds(0, PANEL - 1)])
     residual = (solved_all[p].astype(F32) - total(pull)).astype(BF16)
-    for n in range(8):
-        leafo_out[n] = dot(inverse_t[n * 256:(n + 1) * 256, :], residual).astype(BF16)
+    for k in panel_order:
+        q = lax.rem(p + k, PANEL)
+        rows = pl.ds(pl.multiple_of(q * 256, 256), 256)
+        leafo_out[q] = dot(inverse_t[rows, :], residual).astype(BF16)
+        if k:
+            send("OUT", leafo_out.at[q], leafo.at[p], (l, q))
     leafo[p] = leafo_out[p]
-    to_panel("OUT", lambda q: leafo_out.at[q], leafo.at[p])
     arrived("OUT", leafo.at[pl.ds(0, PANEL - 1)])
     leaf_out[...] = total(leafo).astype(BF16)
 
@@ -539,9 +561,9 @@
     sems = pltpu.SemaphoreType.DMA((len(X),))
     scratch = [
         bf(256, 2048), bf(3, 512, 2048), bf(512, 512), bf(4, 256, 512), bf(4, 128, 512),
-        bf(512, 512), bf(512, 512), bf(4, 512, 256), pltpu.SemaphoreType.DMA((10,)), sems, sems,
+        bf(512, 512), bf(512, 512), bf(4, 512, 256), pltpu.SemaphoreType.DMA((11,)), sems, sems,
         pltpu.SemaphoreType.DMA((2, 4)), pltpu.SemaphoreType.DMA((8,)), pltpu.SemaphoreType.DMA, pltpu.SemaphoreType.REGULAR((3,)),
-        pieces(8, 256), bf(7, 16, 128), pieces(32, 16), pieces(8, 256), pieces(32, 16), pieces(32, 16),
+        pieces(8, 256), bf(7, 16, 128), pltpu.SMEM((3, 1, 32), jnp.int32), pieces(32, 16), pieces(8, 256), pieces(32, 16), pieces(32, 16),
         f32(512, 128), f32(512, 128), f32(512, 128),
         pieces(4, 16), pieces(32, 16), pieces(8, 64), pieces(8, 64), pieces(8, 64),
         pieces(32, 32), pieces(32, 32), pieces(16, 32), pieces(16, 32),
@@ -558,14 +580,14 @@
     return pl.pallas_call(
         kernel,
         out_shape=(jax.ShapeDtypeStruct((256, 128), BF16), jax.ShapeDtypeStruct((7, 16, 128), BF16)),
-        in_specs=[smem, smem, hbm, hbm, hbm, hbm, hbm, hbm, hbm, hbm, hbm, hbm],
+        in_specs=[smem, hbm, hbm, hbm, hbm, hbm, hbm, hbm, hbm, hbm, hbm, hbm],
         out_specs=(vmem, vmem),
         scratch_shapes=scratch,
         compiler_params=pltpu.CompilerParams(collective_id=0, has_side_effects=True, vmem_limit_bytes=VMEM_BYTES),
         cost_estimate=pl.CostEstimate(flops=2_400_000_000, bytes_accessed=12_000_000, transcendentals=0),
         name="solve",
     )(
-        parent_map, tile_mask, leaf_sides, leaf_inverse, leaf_panels, top_sides,
+        parent_map, tile_mask.transpose(1, 0, 2), leaf_sides, leaf_inverse, leaf_panels, top_sides,
         grand_inverse, child_inverse, root_inverse, child_panels, root_grand, root_child,
     )
 

time: 168 us -> 165 us (0.982)
    unnamed x3 -> x2, local copies, waits for them, and re-layouts: 4.09 us -> 2.83 us
where the time goes in v3:
time: 165 us
  Pallas kernels  161 us (98%)
  local copies, waits for them, and re-layouts  2.83 us (2%)
    pallas_call x1, Pallas kernels, per_device(): pl.pallas_call(kernel, out_shape=(jax.ShapeDtypeStruct((256, 128), BF16),...  161 us

profile of v3, /device:TPU:1, one launch (start us, length us, event | category | flops | bytes accessed | tf_op | source)
XLA Modules:
  0.0 164.8 jit_solution(1905753577653003873)
XLA Ops:
  1.3 160.6 %solve.1 = (bf16[256,128]{1,0:T(8,128)(2,1)}, bf16[7,16,128]{2,1,0:T(8,128)(2,1)}) custom-call(s32[1]{0:T(128)S(6)} %copy.16.parent, s32[3,1,32]{2,1,0:T(1,128)} %bitcast.1, bf16[256,128]{1,0:T(8,128)(2,1)} %sides_h.1, bf16[256,2048]{1,0:T(8,128)(2,1)} %inverse_h.1, bf16[3,512,2048]{2,1,0:T(8,128)(2,1)} %panels_h.1, bf16[7,16,128]{2,1,0:T(8,128)(2,1)} %tops_h.1, ...), custom_call_target="tpu_custom_call" | custom-call | flops 2400000000 | bytes 12000000 | tf_op jit(solution)/shard_map/solve/pallas_call | solution.py:580
  161.9 1.5 copy.17
  163.4 1.4 copy.18

commit v4 on v3

--- a/solution.py
+++ b/solution.py
@@ -583,7 +583,7 @@
         in_specs=[smem, hbm, hbm, hbm, hbm, hbm, hbm, hbm, hbm, hbm, hbm, hbm],
         out_specs=(vmem, vmem),
         scratch_shapes=scratch,
-        compiler_params=pltpu.CompilerParams(collective_id=0, has_side_effects=True, vmem_limit_bytes=VMEM_BYTES),
+        compiler_params=pltpu.CompilerParams(collective_id=0, has_side_effects=True, vmem_limit_bytes=VMEM_BYTES, fuse_transposed_lhs_in_matmul=True),
         cost_estimate=pl.CostEstimate(flops=2_400_000_000, bytes_accessed=12_000_000, transcendentals=0),
         name="solve",
     )(

time: 165 us -> 165 us (level)
  no operation moved by 1% of the time
where the time goes in v4:
time: 165 us
  Pallas kernels  161 us (98%)
  local copies, waits for them, and re-layouts  2.83 us (2%)
    pallas_call x1, Pallas kernels, per_device(): pl.pallas_call(kernel, out_shape=(jax.ShapeDtypeStruct((256, 128), BF16),...  161 us

profile of v4, /device:TPU:1, one launch (start us, length us, event | category | flops | bytes accessed | tf_op | source)
XLA Modules:
  0.0 164.8 jit_solution(13981112804962146413)
XLA Ops:
  1.3 160.7 %solve.1 = (bf16[256,128]{1,0:T(8,128)(2,1)}, bf16[7,16,128]{2,1,0:T(8,128)(2,1)}) custom-call(s32[1]{0:T(128)S(6)} %copy.16.parent, s32[3,1,32]{2,1,0:T(1,128)} %bitcast.1, bf16[256,128]{1,0:T(8,128)(2,1)} %sides_h.1, bf16[256,2048]{1,0:T(8,128)(2,1)} %inverse_h.1, bf16[3,512,2048]{2,1,0:T(8,128)(2,1)} %panels_h.1, bf16[7,16,128]{2,1,0:T(8,128)(2,1)} %tops_h.1, ...), custom_call_target="tpu_custom_call" | custom-call | flops 2400000000 | bytes 12000000 | tf_op jit(solution)/shard_map/solve/pallas_call | solution.py:580
  162.0 1.5 copy.17
  163.5 1.4 copy.18
